TPU v7x, 256 devices: a whole 4x4x8 slice. The times are simulated.
256 devices in a mesh: dp: 4 (over x_hi, core), row: 8 (over z), col: 8 (over x_lo, y).
Axes of the slice: x: 4 (x_hi: 2, x_lo: 2; x = x_hi * 2 + x_lo), y: 4, z: 8, core: 2. Of those that a mesh axis runs over, the one named last changes fastest.
Arguments:
- pair_rep: bfloat16 [4096, 1024, 128], P(('dp', 'row'), 'col'), parts along dimension 0, may hold values from -6 to 6
- pair_mask: int32 [4096, 1024], P(('dp', 'row'), 'col'), parts along dimension 0, may hold values from 0 to 1, as said below
- w_left_gate: bfloat16 [128, 128], replicated, may hold values from -0.5 to 0.5
- w_left_proj: bfloat16 [128, 128], replicated, may hold values from -0.5 to 0.5
- w_right_gate: bfloat16 [128, 128], replicated, may hold values from -0.5 to 0.5
- w_right_proj: bfloat16 [128, 128], replicated, may hold values from -0.5 to 0.5
- w_gate: bfloat16 [128, 128], replicated, may hold values from -0.5 to 0.5
- w_out: bfloat16 [128, 128], replicated, may hold values from -0.5 to 0.5
Outputs:
- update: bfloat16 [4096, 1024, 128], P(('dp', 'row'), 'col'), parts along dimension 0
There are 4 independent parts, one for each index of `dp`. A program takes and returns all parts, laid end to end along the dimension named above; an argument that names none is the same for every part. Nothing has to cross between parts.
Inputs may be any that keep to these rules, and one draw needn't show every extreme that they name: pair_mask[i,k] = valid[i] * valid[k] for a 0/1 vector valid over the 1024 tokens of the crop; exactly 256 tokens are invalid.
All inputs are finite; a program needn't handle non-finite values.
Results may differ from a plain program's by a relative error of at most 0.0083.
Values may be sent and summed in bfloat16 or wider, within the bound.
A program may use at most 128 MiB of HBM per device.

v0:
```python
import jax
import jax.numpy as jnp
from jax import lax
from jax.sharding import PartitionSpec as P


def normalize(values, along):
    average = jnp.mean(values, along, keepdims=True)
    centre = values - average
    spread = jnp.mean(centre * centre, along, keepdims=True)
    return centre * lax.rsqrt(spread + 1e-05)


def on_device(
    pair_rep, pair_mask, w_left_gate, w_left_proj, w_right_gate, w_right_proj, w_gate, w_out
):
    tile_rows, tile_cols, pair_width = pair_rep.shape
    channels = w_left_gate.shape[1]
    grid_rows = lax.axis_size("row")
    grid_cols = lax.axis_size("col")
    per_device = channels // (grid_rows * grid_cols)
    cells = tile_rows * tile_cols
    normed = (
        normalize(pair_rep.astype(jnp.float32), 2).astype(jnp.bfloat16).reshape(cells, pair_width)
    )
    weight = pair_mask.astype(jnp.float32).reshape(1, cells)

    def project(gate_matrix, proj_matrix):
        gate_term = jnp.einsum("nd,dc->cn", normed, gate_matrix, preferred_element_type=jnp.float32)
        proj_term = jnp.einsum("nd,dc->cn", normed, proj_matrix, preferred_element_type=jnp.float32)
        edges = jax.nn.sigmoid(gate_term) * proj_term * weight
        return edges.astype(jnp.bfloat16).reshape(channels, tile_rows, tile_cols)

    left_side = project(w_left_gate, w_left_proj)
    right_side = project(w_right_gate, w_right_proj)
    gate_values = jax.nn.sigmoid(jnp.dot(normed, w_gate, preferred_element_type=jnp.float32))
    left_all, right_all = (
        lax.all_to_all(
            lax.all_to_all(left_side, "row", split_axis=0, concat_axis=1, tiled=True),
            "col",
            split_axis=0,
            concat_axis=2,
            tiled=True,
        ),
        lax.all_to_all(
            lax.all_to_all(right_side, "row", split_axis=0, concat_axis=1, tiled=True),
            "col",
            split_axis=0,
            concat_axis=2,
            tiled=True,
        ),
    )
    product = jnp.einsum(
        "cik,cjk->cij", left_all, right_all, preferred_element_type=jnp.float32
    ).astype(jnp.bfloat16)
    back_tiles = lax.all_to_all(
        lax.all_to_all(product, "row", split_axis=1, concat_axis=0, tiled=True),
        "col",
        split_axis=2,
        concat_axis=0,
        tiled=True,
    ).reshape(channels, cells)
    out_rows = (
        w_out.reshape(grid_rows, grid_cols, per_device, pair_width)
        .transpose(1, 0, 2, 3)
        .reshape(channels, pair_width)
    )
    mixed_norm = normalize(back_tiles.astype(jnp.float32), 0).astype(jnp.bfloat16)
    update = gate_values * jnp.einsum(
        "cn,cd->nd", mixed_norm, out_rows, preferred_element_type=jnp.float32
    )
    return update.astype(jnp.bfloat16).reshape(tile_rows, tile_cols, pair_width)


def solution(mesh):
    in_specs = (
        P(("dp", "row"), "col", None),
        P(("dp", "row"), "col"),
        P(),
        P(),
        P(),
        P(),
        P(),
        P(),
    )
    out_specs = P(("dp", "row"), "col", None)
    return jax.shard_map(
        on_device, mesh=mesh, in_specs=in_specs, out_specs=out_specs, check_vma=False
    )
```

profile of v0, /device:TPU:4, one launch (start us, length us, event | category | flops | bytes accessed | tf_op | source)
XLA Modules:
  0.0 544.0 jit_solution(8730875906622245480)
XLA Ops:
  0.0 0.0 copy-start
  0.0 0.0 copy-start.5
  0.0 3.5 convert_reduce_fusion
  3.5 0.0 copy-done.5
  3.5 4.8 fusion.16
  8.3 0.0 copy-start.6
  8.4 4.9 fusion.17
  13.3 0.0 copy-done.6
  13.3 0.0 copy-start.3
  13.3 0.0 copy-done
  13.3 0.0 copy-start.8
  13.3 2.4 fusion.12
  15.7 0.0 copy-done.3
  15.7 0.0 copy-done.8
  15.7 8.0 %fusion.8 = bf16[16384,128]{1,0:T(8,128)(2,1)} fusion(f32[16384,128]{1,0:T(8,128)S(1)} %fusion.12, bf16[16384,128]{1,0:T(8,128)(2,1)S(1)} %bitcast.70, bf16[128,128]{1,0:T(8,128)(2,1)S(1)} %copy-done.8, f32[16384]{0:T(1024)S(1)} %convert_bitcast_fusion), kind=kOutput, calls=%fused_computation.14 | convolution fusion | flops 543162368 | bytes 16875520 | tf_op jit(solution)/shard_map/nd,dc->cn/dot_general | solution.py:30
  23.7 6.8 %copy.28 = bf16[128,128,128]{2,1,0:T(8,128)(2,1)} copy(bf16[128,128,128]{0,2,1:T(8,128)(2,1)} %bitcast.76) | data formatting | bytes 8388608 | tf_op jit(solution)/shard_map/reshape | solution.py:32
  30.5 0.0 copy-start.10
  30.5 8.6 %all-to-all-start = ((bf16[128,128,128]{2,1,0:T(8,128)(2,1)}), bf16[128,128,128]{2,1,0:T(8,128)(2,1)}, u32[]{:S(2)}, u32[]{:S(2)}) async-start(bf16[128,128,128]{2,1,0:T(8,128)(2,1)} %copy.28), calls=%async_computation | async-start | bytes 8388608 | tf_op jit(solution)/shard_map/all_to_all | solution.py:39
  39.1 0.0 copy-done.10
  39.1 0.0 copy-start.4
  39.1 0.0 copy-start.9
  39.1 4.7 fusion.11
  43.8 0.0 copy-done.4
  43.8 0.0 copy-done.9
  43.8 8.1 %fusion.9 = bf16[16384,128]{1,0:T(8,128)(2,1)} fusion(f32[16384,128]{1,0:T(8,128)S(1)} %fusion.11, bf16[16384,128]{1,0:T(8,128)(2,1)S(1)} %bitcast.73, bf16[128,128]{1,0:T(8,128)(2,1)S(1)} %copy-done.9, f32[16384]{0:T(1024)S(1)} %convert_bitcast_fusion), kind=kOutput, calls=%fused_computation.15 | convolution fusion | flops 543162368 | bytes 16875520 | tf_op jit(solution)/shard_map/nd,dc->cn/dot_general | solution.py:30
  51.9 6.6 %copy.31 = bf16[128,128,128]{2,1,0:T(8,128)(2,1)} copy(bf16[128,128,128]{0,2,1:T(8,128)(2,1)} %bitcast.75) | data formatting | bytes 8388608 | tf_op jit(solution)/shard_map/reshape | solution.py:32
  58.5 77.0 %all-to-all-done = bf16[128,128,128]{2,1,0:T(8,128)(2,1)} async-done(((bf16[128,128,128]{2,1,0:T(8,128)(2,1)}), bf16[128,128,128]{2,1,0:T(8,128)(2,1)}, u32[]{:S(2)}, u32[]{:S(2)}) %all-to-all-start) | async-done | bytes 4194336 | tf_op jit(solution)/shard_map/all_to_all | solution.py:39
  135.5 4.7 all-to-all-start.2
  140.2 4.7 copy.29
  144.9 87.4 %all-to-all-done.2 = bf16[128,128,128]{2,1,0:T(8,128)(2,1)} async-done(((bf16[128,128,128]{2,1,0:T(8,128)(2,1)}), bf16[128,128,128]{2,1,0:T(8,128)(2,1)}, u32[]{:S(2)}, u32[]{:S(2)}) %all-to-all-start.2) | async-done | bytes 4194336 | tf_op jit(solution)/shard_map/all_to_all | solution.py:46
  232.3 5.1 all-to-all-start.1
  237.4 4.7 copy.32
  242.1 44.0 %all-to-all-done.1 = bf16[16,1024,128]{2,1,0:T(8,128)(2,1)} async-done(((bf16[16,1024,128]{2,1,0:T(8,128)(2,1)}), bf16[16,1024,128]{2,1,0:T(8,128)(2,1)}, u32[]{:S(2)}, u32[]{:S(2)}) %all-to-all-start.1) | async-done | bytes 4194336 | tf_op jit(solution)/shard_map/all_to_all | solution.py:38
  286.1 53.8 %all_to_all.99 = bf16[16,1024,128]{2,1,0:T(8,128)(2,1)S(1)} all-to-all(bf16[16,1024,128]{2,1,0:T(8,128)(2,1)} %bitcast.80), channel_id=1, replica_groups=mesh['dp'=4,'row'=8,'col'=8] {'col'}, dimensions={0} | all-to-all | bytes 8388608 | tf_op jit(solution)/shard_map/all_to_all | solution.py:45
  339.9 8.4 %fusion.25 = bf16[2,1024,1024]{2,1,0:T(8,128)(2,1)} fusion(bf16[8,2,128,8,128]{4,3,2,1,0:T(8,128)(2,1)S(1)} %bitcast.83, bf16[8,2,128,8,128]{4,3,2,1,0:T(8,128)(2,1)} %bitcast.34), kind=kOutput, calls=%fused_computation.37 | convolution fusion | flops 4297064448 | bytes 12582912 | tf_op jit(solution)/shard_map/cik,cjk->cij/dot_general | solution.py:53
  348.2 6.5 %copy.34 = bf16[2,1024,1024]{2,0,1:T(2,128)(2,1)S(1)} copy(bf16[2,1024,1024]{2,1,0:T(8,128)(2,1)} %fusion.25) | data formatting | bytes 8388608 | tf_op jit(solution)/shard_map/convert_element_type | solution.py:55
  354.7 100.6 %all_to_all.100 = bf16[2,1024,1024]{2,0,1:T(2,128)(2,1)S(1)} all-to-all(bf16[2,1024,1024]{2,0,1:T(2,128)(2,1)S(1)} %copy.34), channel_id=1, replica_groups=mesh['dp'=4,'row'=8,'col'=8] {'row'}, dimensions={1} | all-to-all | bytes 8388608 | tf_op jit(solution)/shard_map/all_to_all | solution.py:57
  455.3 1.3 copy.35
  456.6 2.4 copy.36
  459.0 7.0 %copy.37 = bf16[16,128,1024]{1,0,2:T(8,128)(2,1)} copy(bf16[16,128,1024]{2,1,0:T(8,128)(2,1)} %bitcast.82) | data formatting | bytes 8388608 | tf_op jit(solution)/shard_map/all_to_all | solution.py:57
  466.0 0.0 copy-start.7
  466.0 0.0 copy-start.11
  466.0 4.7 all-to-all-start.5
  470.7 0.0 copy-done.7
  470.7 0.0 copy-done.11
  470.7 7.8 %fusion.13 = f32[16384,128]{1,0:T(8,128)} fusion(bf16[16384,128]{1,0:T(8,128)(2,1)} %bitcast.72, bf16[128,128]{1,0:T(8,128)(2,1)S(1)} %copy-done.11), kind=kOutput, calls=%fused_computation.19 | convolution fusion | flops 543162368 | bytes 12615680 | tf_op jit(solution)/shard_map/dot_general | solution.py:36
  478.5 37.5 %all-to-all-done.5 = bf16[16,128,1024]{1,0,2:T(8,128)(2,1)} async-done(((bf16[16,128,1024]{1,0,2:T(8,128)(2,1)}), bf16[16,128,1024]{1,0,2:T(8,128)(2,1)}, u32[]{:S(2)}, u32[]{:S(2)}) %all-to-all-start.5) | async-done | bytes 4194336 | tf_op jit(solution)/shard_map/all_to_all | solution.py:56
  516.0 7.8 %copy.38 = f32[16,128,8,128]{3,1,0,2:T(8,128)} copy(bf16[16,128,8,128]{1,0,3,2:T(8,128)(2,1)} %bitcast.32) | data formatting | bytes 12582912 | tf_op jit(solution)/shard_map/convert_element_type | solution.py:68
  523.8 0.0 copy-start.2
  523.8 4.0 bitcast_reduce_fusion
  527.8 1.8 copy-done.2
  529.6 0.0 slice-start
  529.6 0.9 multiply_reduce_fusion
  530.5 0.0 slice-start.1
  530.5 1.3 multiply_convert_fusion
  531.8 0.0 slice-done
  531.8 1.5 slice-done.1
  533.3 0.0 copy-start.1
  533.3 10.7 %fusion.10 = bf16[16384,128]{1,0:T(8,128)(2,1)} fusion(f32[16384,128]{1,0:T(8,128)S(1)} %bitcast.78, bf16[128,128]{1,0:T(8,128)(2,1)S(1)} %bitcast.84, bf16[16,8,128,128]{3,2,1,0:T(8,128)(2,1)S(1)} %bitcast.74), kind=kOutput, calls=%fused_computation.16 | convolution fusion | flops 541065216 | bytes 16809984 | tf_op jit(solution)/shard_map/cn,cd->nd/dot_general | solution.py:69
  544.0 0.0 copy-done.1
  (7 shorter events, 0.1 us)
Async XLA Ops:
  0.0 13.3 %copy-start = (bf16[128,128]{1,0:T(8,128)(2,1)S(1)}, bf16[128,128]{1,0:T(8,128)(2,1)}, u32[]{:S(2)}) copy-start(bf16[128,128]{1,0:T(8,128)(2,1)} %param.10) | copy-start | bytes 98308
  0.0 3.5 copy-start.5
  8.3 4.9 copy-start.6
  13.3 2.4 copy-start.3
  13.3 2.4 copy-start.8
  30.5 8.6 %copy-start.10 = (bf16[128,128]{1,0:T(8,128)(2,1)S(1)}, bf16[128,128]{1,0:T(8,128)(2,1)}, u32[]{:S(2)}) copy-start(bf16[128,128]{1,0:T(8,128)(2,1)} %param.12) | copy-start | bytes 98308
  30.5 105.0 %all-to-all-start = ((bf16[128,128,128]{2,1,0:T(8,128)(2,1)}), bf16[128,128,128]{2,1,0:T(8,128)(2,1)}, u32[]{:S(2)}, u32[]{:S(2)}) async-start(bf16[128,128,128]{2,1,0:T(8,128)(2,1)} %copy.28), calls=%async_computation | async-start | bytes 8388608 | tf_op jit(solution)/shard_map/all_to_all | solution.py:39
  39.1 4.7 copy-start.4
  39.1 4.7 copy-start.9
  135.5 96.8 %all-to-all-start.2 = ((bf16[128,128,128]{2,1,0:T(8,128)(2,1)}), bf16[128,128,128]{2,1,0:T(8,128)(2,1)}, u32[]{:S(2)}, u32[]{:S(2)}) async-start(bf16[128,128,128]{2,1,0:T(8,128)(2,1)} %copy.31), calls=%async_computation.2 | async-start | bytes 8388608 | tf_op jit(solution)/shard_map/all_to_all | solution.py:46
  232.3 53.8 %all-to-all-start.1 = ((bf16[16,1024,128]{2,1,0:T(8,128)(2,1)}), bf16[16,1024,128]{2,1,0:T(8,128)(2,1)}, u32[]{:S(2)}, u32[]{:S(2)}) async-start(bf16[16,1024,128]{2,1,0:T(8,128)(2,1)} %bitcast.79), calls=%async_computation.1 | async-start | bytes 8388608 | tf_op jit(solution)/shard_map/all_to_all | solution.py:38
  466.0 4.7 copy-start.7
  466.0 4.8 copy-start.11
  466.0 50.0 %all-to-all-start.5 = ((bf16[16,128,1024]{1,0,2:T(8,128)(2,1)}), bf16[16,128,1024]{1,0,2:T(8,128)(2,1)}, u32[]{:S(2)}, u32[]{:S(2)}) async-start(bf16[16,128,1024]{1,0,2:T(8,128)(2,1)} %copy.37), calls=%async_computation.5 | async-start | bytes 8388608 | tf_op jit(solution)/shard_map/all_to_all | solution.py:56
  523.8 5.8 %copy-start.2 = (f32[16,128,8,128]{3,1,0,2:T(8,128)S(1)}, f32[16,128,8,128]{3,1,0,2:T(8,128)}, u32[]{:S(2)}) copy-start(f32[16,128,8,128]{3,1,0,2:T(8,128)} %copy.38) | copy-start | bytes 25165828
  529.6 2.2 slice-start
  530.5 2.8 slice-start.1
  533.3 10.7 %copy-start.1 = (bf16[128,128]{1,0:T(8,128)(2,1)S(1)}, bf16[128,128]{1,0:T(8,128)(2,1)}, u32[]{:S(2)}) copy-start(bf16[128,128]{1,0:T(8,128)(2,1)} %param.10) | copy-start | bytes 98308
where the time goes:
time: 546 us; the launch traced here: 544 us
  waiting for transfers between devices  246 us (45%)
  blocking collectives  154 us (28%)
  local copies, waits for them, and re-layouts  51.1 us (9%)
  matrix products  49.9 us (9%)
  starting transfers between devices  23.1 us (4%)
  other arithmetic  19.4 us (4%)
    all_to_all x1, blocking collectives, on_device(): lax.all_to_all(product, 'row', split_axis=1, concat_axis=0, tiled=True)  101 us
    all_to_all x1, waiting for transfers between devices, on_device(): lax.all_to_all(right_side, 'row', split_axis=0, concat_axis=1, tiled=True)  87.4 us
    all_to_all x1, waiting for transfers between devices, on_device(): lax.all_to_all(left_side, 'row', split_axis=0, concat_axis=1, tiled=True)  77 us
    all_to_all x1, blocking collectives, on_device(): lax.all_to_all(lax.all_to_all(right_side, 'row', split_axis=0, concat_axi...  53.8 us
    all_to_all x1, waiting for transfers between devices, on_device(): lax.all_to_all(lax.all_to_all(left_side, 'row', split_axis=0, concat_axis...  44 us
    all_to_all x1, waiting for transfers between devices, on_device(): lax.all_to_all(lax.all_to_all(product, 'row', split_axis=1, concat_axis=0...  37.5 us
    dot_general x2, matrix products, project(): jnp.einsum('nd,dc->cn', normed, proj_matrix, preferred_element_type=jnp.f...  16.1 us
    reshape x2, local copies, waits for them, and re-layouts, project(): return edges.astype(jnp.bfloat16).reshape(channels, tile_rows, tile_cols)  13.4 us
  transfers between devices with their start and end apart: 4, of which 4 were waited for; matrix products, arithmetic and copies ran while one was open for 7% of the time, Pallas kernels for 0%

commit v1 on v0

v1 whole, which is shorter than its diff:
```python
import functools

import jax
import jax.numpy as jnp
from jax import lax
from jax.experimental import pallas as pl
from jax.experimental.pallas import tpu as pltpu
from jax.sharding import PartitionSpec as P

MESH = pl.DeviceIdType.MESH
EPS = 1e-05
VALID = 768
BF = jnp.bfloat16
F32 = jnp.float32


def dot(a, b):
    return jnp.dot(a, b, preferred_element_type=F32)


def dot_t(a, b):
    return lax.dot_general(a, b, (((1,), (1,)), ((), ())), preferred_element_type=F32)


def sigmoid(v):
    return 0.5 * jnp.tanh(0.5 * v) + 0.5


def normalize(v):
    centre = v - jnp.mean(v, axis=0, keepdims=True)
    spread = jnp.mean(centre * centre, axis=0, keepdims=True)
    return centre * lax.rsqrt(spread + EPS)


def wait(ref, sem):
    pltpu.make_async_copy(ref, ref, sem).wait()


def kernel(
    nr, nc, nq,
    x_hbm, mask_ref, wlg_ref, wlp_ref, wrg_ref, wrp_ref, wg_ref, wo_ref,
    out_hbm,
    field, normed, send_r, send_l, recv_r, recv_l, put_r, put_l, got_r, got_l,
    packed_r, prod, back, pick, w_t, maskf, vmine, vrow, vall, perm, eye,
    sem_x, sem_out, sem_v, a_send, a_recv, b_send, br_recv, bl_recv, p_send, p_recv, e_send, e_recv,
):
    row = lax.axis_index("row")
    col = lax.axis_index("col")
    ti, tk = mask_ref.shape
    ch = w_t.shape[1]
    cc = ch // nc
    dc = cc // nr
    qi = ti // nq
    full = nc * tk
    group = 4

    def col_peer(d):
        return lax.rem(col + d, nc)

    def row_peer(d):
        return lax.rem(row + d, nr)

    def x_copy(q):
        part = pl.ds(pl.multiple_of(q * qi, qi), qi)
        return pltpu.make_async_copy(x_hbm.at[part], field.at[part], sem_x.at[q])

    def out_copy(q):
        part = pl.ds(pl.multiple_of(q * qi, qi), qi)
        return pltpu.make_async_copy(send_r.at[part], out_hbm.at[part], sem_out.at[q])

    for q in range(nq):
        x_copy(q).start()

    barrier = pltpu.get_barrier_semaphore()
    for d in range(1, nc):
        pl.semaphore_signal(barrier, inc=1, device_id={"col": col_peer(d)}, device_id_type=MESH)
    for d in range(1, nr):
        pl.semaphore_signal(barrier, inc=1, device_id={"row": row_peer(d)}, device_id_type=MESH)

    eye[...] = (
        lax.broadcasted_iota(jnp.int32, (ch, ch), 0) == lax.broadcasted_iota(jnp.int32, (ch, ch), 1)
    ).astype(F32).astype(BF)
    at = lax.broadcasted_iota(jnp.int32, (cc * 16, cc * 16), 0)
    of = lax.broadcasted_iota(jnp.int32, (cc * 16, cc * 16), 1)
    perm[...] = (of == (at % 16) * cc + at // 16).astype(F32).astype(BF)
    for n, ref in enumerate((wrg_ref, wrp_ref, wlg_ref, wlp_ref, wg_ref, wo_ref)):
        w_t[n] = dot_t(eye[...], ref[...]).astype(BF)
    maskf[...] = mask_ref[...].astype(F32)
    vmine[...] = jnp.broadcast_to(jnp.max(maskf[...], axis=0, keepdims=True), vmine.shape)

    pl.semaphore_wait(barrier, nc - 1 + nr - 1)

    mine = pl.ds(pl.multiple_of(col * tk, tk), tk)
    for d in range(1, nc):
        pltpu.make_async_remote_copy(
            vmine, vrow.at[:, mine], sem_v.at[0], sem_v.at[1],
            device_id={"col": col_peer(d)}, device_id_type=MESH,
        ).start()
    pltpu.make_async_copy(vmine, vrow.at[:, mine], sem_v.at[1]).start()

    def lanes(ref, i):
        return jnp.concatenate([ref[i + g] for g in range(group)], axis=1)

    def edges(n, vals, i, dst):
        g = dot(w_t[n], vals)
        p = dot(w_t[n + 1], vals)
        m = jnp.concatenate([maskf[pl.ds(i + h, 1), :] for h in range(group)], axis=1)
        e = (sigmoid(g) * p * m).astype(BF)
        for h in range(group):
            dst[i + h] = e[:, h * tk:(h + 1) * tk]

    def compute_r(q):
        def body(t, carry):
            i = q * qi + t * group
            x = field[pl.ds(i, group)].reshape(group * tk, ch)
            vals = normalize(dot_t(eye[...], x)).astype(BF)
            for h in range(group):
                normed[i + h] = vals[:, h * tk:(h + 1) * tk]
            edges(0, vals, i, send_r)
            return carry

        lax.fori_loop(0, qi // group, body, 0)

    def compute_l(q):
        def body(t, carry):
            i = q * qi + t * group
            edges(2, lanes(normed, i), i, send_l)
            return carry

        lax.fori_loop(0, qi // group, body, 0)

    def start_a(n, q, src, dst):
        part = pl.ds(pl.multiple_of(q * qi, qi), qi)
        for d in range(1, nc):
            to = col_peer(d)
            pltpu.make_async_remote_copy(
                src.at[part, pl.ds(pl.multiple_of(to * cc, cc), cc), :], dst.at[part, :, mine],
                a_send.at[n, q], a_recv.at[n, q],
                device_id={"col": to}, device_id_type=MESH,
            ).start()
        pltpu.make_async_copy(
            src.at[part, pl.ds(pl.multiple_of(col * cc, cc), cc), :], dst.at[part, :, mine],
            a_recv.at[n, q],
        ).start()

    def compact(n, q, src, dst):
        part = pl.ds(pl.multiple_of(q * qi, qi), qi)
        wait(src.at[part], a_recv.at[n, q])

        def body(t, carry):
            i = pl.multiple_of(q * qi + t * 16, 16)
            a = src[pl.ds(i, 16)].reshape(16 * cc, full)
            b = dot(perm[...], dot_t(a, pick[...]).astype(BF)).astype(BF)
            dst[:, pl.ds(i, 16), :] = b.reshape(cc, 16, VALID)
            return carry

        lax.fori_loop(0, qi // 16, body, 0)

    def start_b(n, q, src, dst_at, recv):
        part = pl.ds(pl.multiple_of(q * qi, qi), qi)
        for d in range(1, nr):
            to = row_peer(d)
            pltpu.make_async_remote_copy(
                src.at[pl.ds(to * dc, dc), part, :], dst_at, b_send.at[n, q], recv,
                device_id={"row": to}, device_id_type=MESH,
            ).start()
        pltpu.make_async_copy(src.at[pl.ds(row * dc, dc), part, :], dst_at, recv).start()

    def ranks(v):
        a = lax.broadcasted_iota(jnp.int32, (tk, tk), 0)
        b = lax.broadcasted_iota(jnp.int32, (tk, tk), 1)
        upto = (a <= b).astype(F32).astype(BF)
        ones = jnp.ones((tk, tk), BF)
        base = jnp.zeros((v.shape[0], tk), F32)
        out = []
        for n in range(nc):
            block = v[:, n * tk:(n + 1) * tk]
            block16 = block.astype(BF)
            rank = dot(block16, upto) + base - 1.0
            out.append(jnp.where(block > 0.5, rank, -1.0))
            base = base + dot(block16, ones)
        return jnp.concatenate(out, axis=1)

    def fill_pick(v):
        rank = ranks(v)[0:1, :].astype(jnp.int32)

        def body(t, carry):
            p = pl.multiple_of(t * 16, 16)
            place = lax.broadcasted_iota(jnp.int32, (16, full), 0) + p
            pick[pl.ds(p, 16), :] = (place == rank).astype(F32).astype(BF)
            return carry

        lax.fori_loop(0, VALID // 16, body, 0)

    def step_r(q, carry):
        x_copy(q).wait()
        compute_r(q)
        start_a(0, q, send_r, recv_r)
        return carry

    lax.fori_loop(0, nq, step_r, 0)

    wait(vrow, sem_v.at[1])
    fill_pick(vrow[...])
    for d in range(1, nr):
        pltpu.make_async_remote_copy(
            vrow, vall.at[row], sem_v.at[2], sem_v.at[3],
            device_id={"row": row_peer(d)}, device_id_type=MESH,
        ).start()
    pltpu.make_async_copy(vrow, vall.at[row], sem_v.at[3]).start()

    def step_l(q, carry):
        compute_l(q)
        compact(0, q, recv_r, put_r)
        mine_rows = pl.ds(pl.multiple_of(row * ti + q * qi, qi), qi)
        start_b(0, q, put_r, got_r.at[:, mine_rows, :], br_recv)
        start_a(1, q, send_l, recv_l)
        return carry

    lax.fori_loop(0, nq, step_l, 0)

    def step_c(q, carry):
        compact(1, q, recv_l, put_l)
        start_b(1, q, put_l, got_l.at[q, :, pl.ds(pl.multiple_of(row * qi, qi), qi), :], bl_recv.at[q])
        return carry

    lax.fori_loop(0, nq, step_c, 0)

    wait(vall, sem_v.at[3])
    fill_pick(jnp.max(vall[...], axis=0))
    wait(got_r, br_recv)

    def pack(t, carry):
        p = pl.multiple_of(t * 256, 256)
        for n in range(dc):
            packed_r[n, pl.ds(p, 256), :] = dot(pick[pl.ds(p, 256), :], got_r[n]).astype(BF)
        return carry

    lax.fori_loop(0, VALID // 256, pack, 0)

    def step_p(q, carry):
        wait(got_l.at[q], bl_recv.at[q])
        for n in range(dc):
            prod[q, n] = dot_t(got_l[q, n], packed_r[n]).astype(BF)
        dst = back.at[q, pl.ds(row * dc, dc)]
        for d in range(1, nr):
            to = row_peer(d)
            pltpu.make_async_remote_copy(
                prod.at[q, :, pl.ds(pl.multiple_of(to * qi, qi), qi), :], dst,
                p_send.at[q], p_recv.at[q],
                device_id={"row": to}, device_id_type=MESH,
            ).start()
        pltpu.make_async_copy(
            prod.at[q, :, pl.ds(pl.multiple_of(row * qi, qi), qi), :], dst, p_recv.at[q]
        ).start()
        return carry

    lax.fori_loop(0, nq, step_p, 0)

    def step_e(q, carry):
        part = pl.ds(pl.multiple_of(q * qi, qi), qi)
        wait(send_l.at[pl.ds(0, qi * (nc - 1) // nc)], a_send.at[1, q])
        wait(send_r.at[pl.ds(0, qi * (nc - 1) // nc)], a_send.at[0, q])
        wait(back.at[q], p_recv.at[q])

        def body(t, carry):
            i = pl.multiple_of(q * qi + t * 16, 16)
            a = back[q, :, pl.ds(pl.multiple_of(t * 16, 16), 16), :].reshape(16 * cc, VALID)
            e = dot(dot(perm[...], a).astype(BF), pick[...]).astype(BF)
            for n in range(nc):
                send_l[pl.ds(i, 16), n * cc:(n + 1) * cc, :] = e[:, n * tk:(n + 1) * tk].reshape(16, cc, tk)
            return carry

        lax.fori_loop(0, qi // 16, body, 0)
        dst = field.at[part, pl.ds(pl.multiple_of(col * cc, cc), cc), :]
        for d in range(1, nc):
            to = col_peer(d)
            pltpu.make_async_remote_copy(
                send_l.at[part, pl.ds(pl.multiple_of(to * cc, cc), cc), :], dst,
                e_send.at[q], e_recv.at[q],
                device_id={"col": to}, device_id_type=MESH,
            ).start()
        pltpu.make_async_copy(
            send_l.at[part, pl.ds(pl.multiple_of(col * cc, cc), cc), :], dst, e_recv.at[q]
        ).start()
        return carry

    lax.fori_loop(0, nq, step_e, 0)

    def step_f(q, carry):
        part = pl.ds(pl.multiple_of(q * qi, qi), qi)
        wait(field.at[part], e_recv.at[q])

        def body(t, carry):
            i = q * qi + t * group
            mixed = normalize(lanes(field, i).astype(F32)).astype(BF)
            u = (sigmoid(dot(w_t[4], lanes(normed, i))) * dot(w_t[5], mixed)).astype(BF)
            for h in range(group):
                send_r[i + h] = dot_t(eye[...], u[:, h * tk:(h + 1) * tk]).astype(BF)
            return carry

        lax.fori_loop(0, qi // group, body, 0)
        out_copy(q).start()
        return carry

    lax.fori_loop(0, nq, step_f, 0)

    wait(vrow.at[:, pl.ds(0, full - tk)], sem_v.at[0])
    wait(vall.at[pl.ds(0, nr - 1)], sem_v.at[2])

    def finish(q, carry):
        wait(put_r.at[pl.ds(0, dc * (nr - 1)), pl.ds(0, qi), :], b_send.at[0, q])
        wait(put_l.at[pl.ds(0, dc * (nr - 1)), pl.ds(0, qi), :], b_send.at[1, q])
        wait(prod.at[0, :, pl.ds(0, qi * (nr - 1)), :], p_send.at[q])
        wait(send_l.at[pl.ds(0, qi * (nc - 1) // nc)], e_send.at[q])
        out_copy(q).wait()
        return carry

    lax.fori_loop(0, nq, finish, 0)


def solution(mesh):
    nr, nc = mesh.shape["row"], mesh.shape["col"]
    nq = 4

    def on_device(pair_rep, pair_mask, w_left_gate, w_left_proj, w_right_gate, w_right_proj, w_gate, w_out):
        ti, tk, cz = pair_rep.shape
        ch = w_left_gate.shape[1]
        cc, dc = ch // nc, ch // nc // nr
        qi = ti // nq
        tile = pltpu.VMEM((ti, ch, tk), BF)
        sem = pltpu.SemaphoreType.DMA
        vmem = pl.BlockSpec(memory_space=pltpu.VMEM)
        return pl.pallas_call(
            functools.partial(kernel, nr, nc, nq),
            out_shape=jax.ShapeDtypeStruct(pair_rep.shape, pair_rep.dtype),
            in_specs=[pl.BlockSpec(memory_space=pl.ANY)] + [vmem] * 7,
            out_specs=pl.BlockSpec(memory_space=pl.ANY),
            scratch_shapes=[
                tile, tile, tile, tile,
                pltpu.VMEM((ti, cc, nc * tk), BF), pltpu.VMEM((ti, cc, nc * tk), BF),
                pltpu.VMEM((cc, ti, VALID), BF), pltpu.VMEM((cc, ti, VALID), BF),
                pltpu.VMEM((dc, nr * ti, VALID), BF), pltpu.VMEM((nq, dc, nr * qi, VALID), BF),
                pltpu.VMEM((dc, VALID, VALID), BF),
                pltpu.VMEM((nq, dc, nr * qi, VALID), BF),
                pltpu.VMEM((nq, cc, qi, VALID), BF),
                pltpu.VMEM((VALID, nc * tk), BF),
                pltpu.VMEM((6, ch, cz), BF),
                pltpu.VMEM((ti, tk), F32), pltpu.VMEM((8, tk), F32),
                pltpu.VMEM((8, nc * tk), F32), pltpu.VMEM((nr, 8, nc * tk), F32),
                pltpu.VMEM((16 * cc, 16 * cc), BF), pltpu.VMEM((ch, ch), BF),
                sem((nq,)), sem((nq,)), sem((4,)), sem((2, nq)), sem((2, nq)), sem((2, nq)),
                sem(()), sem((nq,)), sem((nq,)), sem((nq,)), sem((nq,)), sem((nq,)),
            ],
            compiler_params=pltpu.CompilerParams(
                collective_id=0, has_side_effects=True, vmem_limit_bytes=58 << 20
            ),
        )(pair_rep, pair_mask, w_left_gate, w_left_proj, w_right_gate, w_right_proj, w_gate, w_out)

    in_specs = (P(("dp", "row"), "col", None), P(("dp", "row"), "col")) + (P(),) * 6
    return jax.shard_map(
        on_device, mesh=mesh, in_specs=in_specs, out_specs=P(("dp", "row"), "col", None), check_vma=False
    )
```

time: 546 us -> 262 us (0.48)
  Pallas kernels: 0 us -> 255 us
  waiting for transfers between devices: 246 us -> 0 us
  blocking collectives: 154 us -> 0 us
  matrix products: 49.9 us -> 0 us
  local copies, waits for them, and re-layouts: 51.1 us -> 4.79 us
  starting transfers between devices: 23.1 us -> 0 us
  other arithmetic: 19.4 us -> 0 us
    pallas_call x0 -> x1, Pallas kernels: none -> 255 us  [on_device(): pl.pallas_call(functools.partial(kernel, nr, nc, nq), out_shape=jax.Shape...]
    all_to_all x4 -> x0, waiting for transfers between devices: 246 us -> none  [the longest x1 87.4 us: on_device(): lax.all_to_all(right_side, 'row', split_axis=0, concat_axis=1, tiled=True)]
    all_to_all x2 -> x0, blocking collectives: 154 us -> none  [the longest x1 101 us: on_device(): lax.all_to_all(product, 'row', split_axis=1, concat_axis=0, tiled=True)]
    dot_general x7 -> x0, matrix products: 49.9 us -> none  [the longest x2 16.1 us: project(): jnp.einsum('nd,dc->cn', normed, proj_matrix, preferred_element_type=jnp.f...]
    all_to_all x4 -> x0, starting transfers between devices: 23.1 us -> none  [the longest x1 8.59 us: on_device(): lax.all_to_all(left_side, 'row', split_axis=0, concat_axis=1, tiled=True)]
    all_to_all x5 -> x0, local copies, waits for them, and re-layouts: 20.1 us -> none  [the longest x3 10.6 us: on_device(): lax.all_to_all(product, 'row', split_axis=1, concat_axis=0, tiled=True)]
    convert_element_type x2 -> x0, local copies, waits for them, and re-layouts: 14.3 us -> none  [the longest x1 7.79 us: on_device(): back_tiles.astype(jnp.float32)]
    reshape x3 -> x0, local copies, waits for them, and re-layouts: 13.4 us -> none  [the longest x2 13.4 us: project(): return edges.astype(jnp.bfloat16).reshape(channels, tile_rows, tile_cols)]
  transfers between devices with their start and end apart: 4 -> 0, of which waited for: 4 -> 0; matrix products, arithmetic and copies ran while one was open for 7% -> 0% of each run, Pallas kernels for 0% -> 0%
where the time goes in v1:
time: 262 us; the launch traced here: 259 us
  Pallas kernels  255 us (97%)
  local copies, waits for them, and re-layouts  4.79 us (2%)
    pallas_call x1, Pallas kernels, on_device(): pl.pallas_call(functools.partial(kernel, nr, nc, nq), out_shape=jax.Shape...  255 us

profile of v1, /device:TPU:4, one launch (start us, length us, event | category | flops | bytes accessed | tf_op | source)
XLA Modules:
  0.0 259.5 jit_solution(10160627800123698511)
XLA Ops:
  0.0 254.7 %shard_map.82 = bf16[128,128,128]{2,1,0:T(8,128)(2,1)} custom-call(bf16[128,128,128]{2,1,0:T(8,128)(2,1)} %x_hbm.1, s32[128,128]{1,0:T(8,128)} %mask_ref.1, bf16[128,128]{1,0:T(8,128)(2,1)} %wlg_ref.1, bf16[128,128]{1,0:T(8,128)(2,1)} %wlp_ref.1, bf16[128,128]{1,0:T(8,128)(2,1)} %wrg_ref.1, bf16[128,128]{1,0:T(8,128)(2,1)} %wrp_ref.1, ...), custom_call_target="tpu_custom_call" | custom-call | tf_op jit(solution)/shard_map/pallas_call | solution.py:334
  254.7 4.8 %copy.10 = bf16[128,128,128]{2,1,0:T(8,128)(2,1)} copy(bf16[128,128,128]{2,1,0:T(8,128)(2,1)} %shard_map.82) | data formatting | bytes 8388608

commit v2 on v1

--- a/solution.py
+++ b/solution.py
@@ -52,7 +52,7 @@
     dc = cc // nr
     qi = ti // nq
     full = nc * tk
-    group = 4
+    group = 8
 
     def col_peer(d):
         return lax.rem(col + d, nc)
@@ -210,10 +210,10 @@
     pltpu.make_async_copy(vrow, vall.at[row], sem_v.at[3]).start()
 
     def step_l(q, carry):
-        compute_l(q)
         compact(0, q, recv_r, put_r)
         mine_rows = pl.ds(pl.multiple_of(row * ti + q * qi, qi), qi)
         start_b(0, q, put_r, got_r.at[:, mine_rows, :], br_recv)
+        compute_l(q)
         start_a(1, q, send_l, recv_l)
         return carry
 
@@ -321,7 +321,7 @@
 
 def solution(mesh):
     nr, nc = mesh.shape["row"], mesh.shape["col"]
-    nq = 4
+    nq = 8
 
     def on_device(pair_rep, pair_mask, w_left_gate, w_left_proj, w_right_gate, w_right_proj, w_gate, w_out):
         ti, tk, cz = pair_rep.shape

time: 262 us -> 247 us (0.943)
  Pallas kernels: 255 us -> 242 us
    pallas_call x1, Pallas kernels: 255 us -> 242 us  [on_device(): pl.pallas_call(functools.partial(kernel, nr, nc, nq), out_shape=jax.Shape...]
where the time goes in v2:
time: 247 us
  Pallas kernels  242 us (98%)
  local copies, waits for them, and re-layouts  4.79 us (2%)
    pallas_call x1, Pallas kernels, on_device(): pl.pallas_call(functools.partial(kernel, nr, nc, nq), out_shape=jax.Shape...  242 us

profile of v2, /device:TPU:4, one launch (start us, length us, event | category | flops | bytes accessed | tf_op | source)
XLA Modules:
  0.0 246.6 jit_solution(3394025491780102399)
XLA Ops:
  0.0 241.8 %shard_map.82 = bf16[128,128,128]{2,1,0:T(8,128)(2,1)} custom-call(bf16[128,128,128]{2,1,0:T(8,128)(2,1)} %x_hbm.1, s32[128,128]{1,0:T(8,128)} %mask_ref.1, bf16[128,128]{1,0:T(8,128)(2,1)} %wlg_ref.1, bf16[128,128]{1,0:T(8,128)(2,1)} %wlp_ref.1, bf16[128,128]{1,0:T(8,128)(2,1)} %wrg_ref.1, bf16[128,128]{1,0:T(8,128)(2,1)} %wrp_ref.1, ...), custom_call_target="tpu_custom_call" | custom-call | tf_op jit(solution)/shard_map/pallas_call | solution.py:334
  241.8 4.8 %copy.10 = bf16[128,128,128]{2,1,0:T(8,128)(2,1)} copy(bf16[128,128,128]{2,1,0:T(8,128)(2,1)} %shard_map.82) | data formatting | bytes 8388608

commit v3 on v2

--- a/solution.py
+++ b/solution.py
@@ -42,7 +42,7 @@
     out_hbm,
     field, normed, send_r, send_l, recv_r, recv_l, put_r, put_l, got_r, got_l,
     packed_r, prod, back, pick, w_t, maskf, vmine, vrow, vall, perm, eye,
-    sem_x, sem_out, sem_v, a_send, a_recv, b_send, br_recv, bl_recv, p_send, p_recv, e_send, e_recv,
+    sem_x, sem_out, sem_v, a_send, a_recv, b_send, br_recv, f_send, f_recv, bl_recv, p_send, p_recv, e_send, e_recv,
 ):
     row = lax.axis_index("row")
     col = lax.axis_index("col")
@@ -52,13 +52,16 @@
     dc = cc // nr
     qi = ti // nq
     full = nc * tk
+    near = nr // 2
+    ahead = nq // 2
+    lag = 2
     group = 8
 
     def col_peer(d):
         return lax.rem(col + d, nc)
 
     def row_peer(d):
-        return lax.rem(row + d, nr)
+        return lax.rem(row + d + nr, nr)
 
     def x_copy(q):
         part = pl.ds(pl.multiple_of(q * qi, qi), qi)
@@ -88,15 +91,7 @@
     maskf[...] = mask_ref[...].astype(F32)
     vmine[...] = jnp.broadcast_to(jnp.max(maskf[...], axis=0, keepdims=True), vmine.shape)
 
-    pl.semaphore_wait(barrier, nc - 1 + nr - 1)
-
     mine = pl.ds(pl.multiple_of(col * tk, tk), tk)
-    for d in range(1, nc):
-        pltpu.make_async_remote_copy(
-            vmine, vrow.at[:, mine], sem_v.at[0], sem_v.at[1],
-            device_id={"col": col_peer(d)}, device_id_type=MESH,
-        ).start()
-    pltpu.make_async_copy(vmine, vrow.at[:, mine], sem_v.at[1]).start()
 
     def lanes(ref, i):
         return jnp.concatenate([ref[i + g] for g in range(group)], axis=1)
@@ -156,15 +151,71 @@
 
         lax.fori_loop(0, qi // 16, body, 0)
 
-    def start_b(n, q, src, dst_at, recv):
-        part = pl.ds(pl.multiple_of(q * qi, qi), qi)
-        for d in range(1, nr):
-            to = row_peer(d)
+    def start_near(piece, send, recv):
+        for b in range(1, near):
+            for slot_at, d in ((0, b), (1, -b)):
+                src, dst = piece(slot_at, b)
+                pltpu.make_async_remote_copy(
+                    src, dst, send, recv, device_id={"row": row_peer(d)}, device_id_type=MESH
+                ).start()
+
+    def channels(g):
+        return pl.ds(lax.rem(g + nr, nr) * dc, dc)
+
+    def chunk(q):
+        return pl.ds(pl.multiple_of(q * qi, qi), qi)
+
+    def rows_of(r, q):
+        return pl.ds(pl.multiple_of(lax.rem(r + nr, nr) * ti + q * qi, qi), qi)
+
+    def send_right(q):
+        def piece(slot, b):
+            group_at = row + b if slot == 0 else row - b - 1
+            return put_r.at[channels(group_at), chunk(q), :], got_r.at[slot, :, rows_of(row, q), :]
+
+        start_near(piece, b_send.at[0, q], br_recv.at[q])
+        for slot in range(2):
+            src = put_r.at[channels(row - slot), chunk(q), :]
             pltpu.make_async_remote_copy(
-                src.at[pl.ds(to * dc, dc), part, :], dst_at, b_send.at[n, q], recv,
-                device_id={"row": to}, device_id_type=MESH,
+                src, got_r.at[1 - slot, :, rows_of(row, q), :], b_send.at[0, q], f_recv,
+                device_id={"row": row_peer(1 - 2 * slot)}, device_id_type=MESH,
             ).start()
-        pltpu.make_async_copy(src.at[pl.ds(row * dc, dc), part, :], dst_at, recv).start()
+            pltpu.make_async_copy(src, got_r.at[slot, :, rows_of(row, q), :], f_recv).start()
+
+    def forward_right(q):
+        wait(got_r.at[:, :, pl.ds(0, (near - 1) * qi), :], br_recv.at[q])
+        for b in range(1, near):
+            for slot in range(2):
+                rows = rows_of(row - b if slot == 0 else row + b, q)
+                pltpu.make_async_remote_copy(
+                    got_r.at[slot, :, rows, :], got_r.at[1 - slot, :, rows, :], f_send.at[q], f_recv,
+                    device_id={"row": row_peer(1 - 2 * slot)}, device_id_type=MESH,
+                ).start()
+
+    def send_left(q):
+        def piece(slot, b):
+            group_at = row + b if slot == 0 else row - b - 1
+            return put_l.at[channels(group_at), chunk(q), :], got_l.at[q, slot, :, pl.ds(b * qi, qi), :]
+
+        start_near(piece, b_send.at[1, q], bl_recv.at[q])
+        for slot in range(2):
+            pltpu.make_async_copy(
+                put_l.at[channels(row - slot), chunk(q), :], got_l.at[q, slot, :, pl.ds(0, qi), :],
+                bl_recv.at[q],
+            ).start()
+
+    def send_product(q):
+        for b in range(near):
+            for slot in range(2):
+                src = prod.at[q, slot, :, pl.ds(b * qi, qi), :]
+                dst = back.at[q, channels(row - slot)]
+                if b == 0:
+                    pltpu.make_async_copy(src, dst, p_recv.at[q]).start()
+                else:
+                    pltpu.make_async_remote_copy(
+                        src, dst, p_send.at[q], p_recv.at[q],
+                        device_id={"row": row_peer(-b if slot == 0 else b)}, device_id_type=MESH,
+                    ).start()
 
     def ranks(v):
         a = lax.broadcasted_iota(jnp.int32, (tk, tk), 0)
@@ -192,13 +243,36 @@
 
         lax.fori_loop(0, VALID // 16, body, 0)
 
-    def step_r(q, carry):
+    x_copy(0).wait()
+    compute_r(0)
+    pl.semaphore_wait(barrier, nc - 1 + nr - 1)
+    start_a(0, 0, send_r, recv_r)
+
+    for d in range(1, nc):
+        pltpu.make_async_remote_copy(
+            vmine, vrow.at[:, mine], sem_v.at[0], sem_v.at[1],
+            device_id={"col": col_peer(d)}, device_id_type=MESH,
+        ).start()
+    pltpu.make_async_copy(vmine, vrow.at[:, mine], sem_v.at[1]).start()
+
+    def next_r(q):
         x_copy(q).wait()
         compute_r(q)
         start_a(0, q, send_r, recv_r)
-        return carry
-
-    lax.fori_loop(0, nq, step_r, 0)
+
+    def next_l(q):
+        compute_l(q)
+        start_a(1, q, send_l, recv_l)
+
+    def loop(low, high, *steps):
+        def body(q, carry):
+            for step in steps:
+                step(q)
+            return carry
+
+        lax.fori_loop(low, high, body, 0)
+
+    loop(1, ahead, next_r)
 
     wait(vrow, sem_v.at[1])
     fill_pick(vrow[...])
@@ -209,55 +283,42 @@
         ).start()
     pltpu.make_async_copy(vrow, vall.at[row], sem_v.at[3]).start()
 
-    def step_l(q, carry):
+    def across_r(q):
         compact(0, q, recv_r, put_r)
-        mine_rows = pl.ds(pl.multiple_of(row * ti + q * qi, qi), qi)
-        start_b(0, q, put_r, got_r.at[:, mine_rows, :], br_recv)
-        compute_l(q)
-        start_a(1, q, send_l, recv_l)
-        return carry
-
-    lax.fori_loop(0, nq, step_l, 0)
-
-    def step_c(q, carry):
+        send_right(q)
+
+    def across_l(q):
         compact(1, q, recv_l, put_l)
-        start_b(1, q, put_l, got_l.at[q, :, pl.ds(pl.multiple_of(row * qi, qi), qi), :], bl_recv.at[q])
-        return carry
-
-    lax.fori_loop(0, nq, step_c, 0)
+        send_left(q)
+
+    loop(0, nq - ahead, across_r, lambda q: next_r(q + ahead))
+    loop(nq - ahead, nq, across_r, lambda q: next_l(q - ahead), lambda q: forward_right(q - ahead))
+    loop(0, nq - ahead, across_l, lambda q: next_l(q + ahead), lambda q: forward_right(q + ahead))
+    loop(nq - ahead, nq, across_l)
 
     wait(vall, sem_v.at[3])
     fill_pick(jnp.max(vall[...], axis=0))
-    wait(got_r, br_recv)
+    wait(got_r.at[:, :, pl.ds(0, (nr - near + 1) * ti), :], f_recv)
 
     def pack(t, carry):
         p = pl.multiple_of(t * 256, 256)
-        for n in range(dc):
-            packed_r[n, pl.ds(p, 256), :] = dot(pick[pl.ds(p, 256), :], got_r[n]).astype(BF)
+        for slot in range(2):
+            for n in range(dc):
+                packed_r[slot, n, pl.ds(p, 256), :] = dot(pick[pl.ds(p, 256), :], got_r[slot, n]).astype(BF)
         return carry
 
     lax.fori_loop(0, VALID // 256, pack, 0)
 
-    def step_p(q, carry):
+    def product(q):
         wait(got_l.at[q], bl_recv.at[q])
-        for n in range(dc):
-            prod[q, n] = dot_t(got_l[q, n], packed_r[n]).astype(BF)
-        dst = back.at[q, pl.ds(row * dc, dc)]
-        for d in range(1, nr):
-            to = row_peer(d)
-            pltpu.make_async_remote_copy(
-                prod.at[q, :, pl.ds(pl.multiple_of(to * qi, qi), qi), :], dst,
-                p_send.at[q], p_recv.at[q],
-                device_id={"row": to}, device_id_type=MESH,
-            ).start()
-        pltpu.make_async_copy(
-            prod.at[q, :, pl.ds(pl.multiple_of(row * qi, qi), qi), :], dst, p_recv.at[q]
-        ).start()
-        return carry
-
-    lax.fori_loop(0, nq, step_p, 0)
-
-    def step_e(q, carry):
+        for slot in range(2):
+            for n in range(dc):
+                prod[q, slot, n] = dot_t(got_l[q, slot, n], packed_r[slot, n]).astype(BF)
+        send_product(q)
+
+    loop(0, nq, product)
+
+    def expand(q):
         part = pl.ds(pl.multiple_of(q * qi, qi), qi)
         wait(send_l.at[pl.ds(0, qi * (nc - 1) // nc)], a_send.at[1, q])
         wait(send_r.at[pl.ds(0, qi * (nc - 1) // nc)], a_send.at[0, q])
@@ -283,11 +344,8 @@
         pltpu.make_async_copy(
             send_l.at[part, pl.ds(pl.multiple_of(col * cc, cc), cc), :], dst, e_recv.at[q]
         ).start()
-        return carry
-
-    lax.fori_loop(0, nq, step_e, 0)
-
-    def step_f(q, carry):
+
+    def last(q):
         part = pl.ds(pl.multiple_of(q * qi, qi), qi)
         wait(field.at[part], e_recv.at[q])
 
@@ -301,22 +359,23 @@
 
         lax.fori_loop(0, qi // group, body, 0)
         out_copy(q).start()
-        return carry
-
-    lax.fori_loop(0, nq, step_f, 0)
+
+    loop(0, lag, expand)
+    loop(lag, nq, expand, lambda q: last(q - lag))
+    loop(nq - lag, nq, last)
 
     wait(vrow.at[:, pl.ds(0, full - tk)], sem_v.at[0])
     wait(vall.at[pl.ds(0, nr - 1)], sem_v.at[2])
 
-    def finish(q, carry):
-        wait(put_r.at[pl.ds(0, dc * (nr - 1)), pl.ds(0, qi), :], b_send.at[0, q])
-        wait(put_l.at[pl.ds(0, dc * (nr - 1)), pl.ds(0, qi), :], b_send.at[1, q])
-        wait(prod.at[0, :, pl.ds(0, qi * (nr - 1)), :], p_send.at[q])
+    def finish(q):
+        wait(put_r.at[pl.ds(0, dc * 2 * near), pl.ds(0, qi), :], b_send.at[0, q])
+        wait(got_r.at[:, :, pl.ds(0, (near - 1) * qi), :], f_send.at[q])
+        wait(put_l.at[pl.ds(0, dc * 2 * (near - 1)), pl.ds(0, qi), :], b_send.at[1, q])
+        wait(prod.at[0, :, :, pl.ds(0, (near - 1) * qi), :], p_send.at[q])
         wait(send_l.at[pl.ds(0, qi * (nc - 1) // nc)], e_send.at[q])
         out_copy(q).wait()
-        return carry
-
-    lax.fori_loop(0, nq, finish, 0)
+
+    loop(0, nq, finish)
 
 
 def solution(mesh):
@@ -340,9 +399,9 @@
                 tile, tile, tile, tile,
                 pltpu.VMEM((ti, cc, nc * tk), BF), pltpu.VMEM((ti, cc, nc * tk), BF),
                 pltpu.VMEM((cc, ti, VALID), BF), pltpu.VMEM((cc, ti, VALID), BF),
-                pltpu.VMEM((dc, nr * ti, VALID), BF), pltpu.VMEM((nq, dc, nr * qi, VALID), BF),
-                pltpu.VMEM((dc, VALID, VALID), BF),
-                pltpu.VMEM((nq, dc, nr * qi, VALID), BF),
+                pltpu.VMEM((2, dc, nr * ti, VALID), BF), pltpu.VMEM((nq, 2, dc, nr // 2 * qi, VALID), BF),
+                pltpu.VMEM((2, dc, VALID, VALID), BF),
+                pltpu.VMEM((nq, 2, dc, nr // 2 * qi, VALID), BF),
                 pltpu.VMEM((nq, cc, qi, VALID), BF),
                 pltpu.VMEM((VALID, nc * tk), BF),
                 pltpu.VMEM((6, ch, cz), BF),
@@ -350,7 +409,7 @@
                 pltpu.VMEM((8, nc * tk), F32), pltpu.VMEM((nr, 8, nc * tk), F32),
                 pltpu.VMEM((16 * cc, 16 * cc), BF), pltpu.VMEM((ch, ch), BF),
                 sem((nq,)), sem((nq,)), sem((4,)), sem((2, nq)), sem((2, nq)), sem((2, nq)),
-                sem(()), sem((nq,)), sem((nq,)), sem((nq,)), sem((nq,)), sem((nq,)),
+                sem((nq,)), sem((nq,)), sem(()), sem((nq,)), sem((nq,)), sem((nq,)), sem((nq,)), sem((nq,)),
             ],
             compiler_params=pltpu.CompilerParams(
                 collective_id=0, has_side_effects=True, vmem_limit_bytes=58 << 20

time: 247 us -> 231 us (0.935); the launches traced: 247 us -> 227 us
  Pallas kernels: 242 us -> 222 us
    pallas_call x1, Pallas kernels: 242 us -> 222 us  [on_device(): pl.pallas_call(functools.partial(kernel, nr, nc, nq), out_shape=jax.Shape...]
where the time goes in v3:
time: 231 us; the launch traced here: 227 us
  Pallas kernels  222 us (96%)
  local copies, waits for them, and re-layouts  4.79 us (2%)
    pallas_call x1, Pallas kernels, on_device(): pl.pallas_call(functools.partial(kernel, nr, nc, nq), out_shape=jax.Shape...  222 us
    unnamed x1, local copies, waits for them, and re-layouts  4.79 us

profile of v3, /device:TPU:4, one launch (start us, length us, event | category | flops | bytes accessed | tf_op | source)
XLA Modules:
  0.0 226.9 jit_solution(1559364543348984835)
XLA Ops:
  0.0 222.1 %shard_map.82 = bf16[128,128,128]{2,1,0:T(8,128)(2,1)} custom-call(bf16[128,128,128]{2,1,0:T(8,128)(2,1)} %x_hbm.1, s32[128,128]{1,0:T(8,128)} %mask_ref.1, bf16[128,128]{1,0:T(8,128)(2,1)} %wlg_ref.1, bf16[128,128]{1,0:T(8,128)(2,1)} %wlp_ref.1, bf16[128,128]{1,0:T(8,128)(2,1)} %wrg_ref.1, bf16[128,128]{1,0:T(8,128)(2,1)} %wrp_ref.1, ...), custom_call_target="tpu_custom_call" | custom-call | tf_op jit(solution)/shard_map/pallas_call | solution.py:393
  222.1 4.8 %copy.10 = bf16[128,128,128]{2,1,0:T(8,128)(2,1)} copy(bf16[128,128,128]{2,1,0:T(8,128)(2,1)} %shard_map.82) | data formatting | bytes 8388608

commit v4 on v3

--- a/solution.py
+++ b/solution.py
@@ -83,9 +83,10 @@
     eye[...] = (
         lax.broadcasted_iota(jnp.int32, (ch, ch), 0) == lax.broadcasted_iota(jnp.int32, (ch, ch), 1)
     ).astype(F32).astype(BF)
-    at = lax.broadcasted_iota(jnp.int32, (cc * 16, cc * 16), 0)
-    of = lax.broadcasted_iota(jnp.int32, (cc * 16, cc * 16), 1)
-    perm[...] = (of == (at % 16) * cc + at // 16).astype(F32).astype(BF)
+    at = lax.broadcasted_iota(jnp.int32, (cc * qi, cc * qi), 0)
+    of = lax.broadcasted_iota(jnp.int32, (cc * qi, cc * qi), 1)
+    perm[0] = (of == (at % qi) * cc + at // qi).astype(F32).astype(BF)
+    perm[1] = (at == (of % qi) * cc + of // qi).astype(F32).astype(BF)
     for n, ref in enumerate((wrg_ref, wrp_ref, wlg_ref, wlp_ref, wg_ref, wo_ref)):
         w_t[n] = dot_t(eye[...], ref[...]).astype(BF)
     maskf[...] = mask_ref[...].astype(F32)
@@ -142,14 +143,9 @@
         part = pl.ds(pl.multiple_of(q * qi, qi), qi)
         wait(src.at[part], a_recv.at[n, q])
 
-        def body(t, carry):
-            i = pl.multiple_of(q * qi + t * 16, 16)
-            a = src[pl.ds(i, 16)].reshape(16 * cc, full)
-            b = dot(perm[...], dot_t(a, pick[...]).astype(BF)).astype(BF)
-            dst[:, pl.ds(i, 16), :] = b.reshape(cc, 16, VALID)
-            return carry
-
-        lax.fori_loop(0, qi // 16, body, 0)
+        a = src[part].reshape(qi * cc, full)
+        b = dot(perm[0], dot_t(a, pick[...]).astype(BF)).astype(BF)
+        dst[q] = b.reshape(nr, dc * qi, VALID)
 
     def start_near(piece, send, recv):
         for b in range(1, near):
@@ -159,56 +155,49 @@
                     src, dst, send, recv, device_id={"row": row_peer(d)}, device_id_type=MESH
                 ).start()
 
-    def channels(g):
-        return pl.ds(lax.rem(g + nr, nr) * dc, dc)
-
-    def chunk(q):
-        return pl.ds(pl.multiple_of(q * qi, qi), qi)
-
-    def rows_of(r, q):
-        return pl.ds(pl.multiple_of(lax.rem(r + nr, nr) * ti + q * qi, qi), qi)
+    def ring(r):
+        return lax.rem(r + nr, nr)
 
     def send_right(q):
         def piece(slot, b):
             group_at = row + b if slot == 0 else row - b - 1
-            return put_r.at[channels(group_at), chunk(q), :], got_r.at[slot, :, rows_of(row, q), :]
+            return put_r.at[q, ring(group_at)], got_r.at[slot, row, q]
 
         start_near(piece, b_send.at[0, q], br_recv.at[q])
         for slot in range(2):
-            src = put_r.at[channels(row - slot), chunk(q), :]
+            src = put_r.at[q, ring(row - slot)]
             pltpu.make_async_remote_copy(
-                src, got_r.at[1 - slot, :, rows_of(row, q), :], b_send.at[0, q], f_recv,
+                src, got_r.at[1 - slot, row, q], b_send.at[0, q], f_recv,
                 device_id={"row": row_peer(1 - 2 * slot)}, device_id_type=MESH,
             ).start()
-            pltpu.make_async_copy(src, got_r.at[slot, :, rows_of(row, q), :], f_recv).start()
+            pltpu.make_async_copy(src, got_r.at[slot, row, q], f_recv).start()
 
     def forward_right(q):
-        wait(got_r.at[:, :, pl.ds(0, (near - 1) * qi), :], br_recv.at[q])
+        wait(put_r.at[0, pl.ds(0, 2 * (near - 1))], br_recv.at[q])
         for b in range(1, near):
             for slot in range(2):
-                rows = rows_of(row - b if slot == 0 else row + b, q)
+                r = ring(row - b if slot == 0 else row + b)
                 pltpu.make_async_remote_copy(
-                    got_r.at[slot, :, rows, :], got_r.at[1 - slot, :, rows, :], f_send.at[q], f_recv,
+                    got_r.at[slot, r, q], got_r.at[1 - slot, r, q], f_send.at[q], f_recv,
                     device_id={"row": row_peer(1 - 2 * slot)}, device_id_type=MESH,
                 ).start()
 
     def send_left(q):
         def piece(slot, b):
             group_at = row + b if slot == 0 else row - b - 1
-            return put_l.at[channels(group_at), chunk(q), :], got_l.at[q, slot, :, pl.ds(b * qi, qi), :]
+            return put_l.at[q, ring(group_at)], got_l.at[q, slot, b]
 
         start_near(piece, b_send.at[1, q], bl_recv.at[q])
         for slot in range(2):
             pltpu.make_async_copy(
-                put_l.at[channels(row - slot), chunk(q), :], got_l.at[q, slot, :, pl.ds(0, qi), :],
-                bl_recv.at[q],
+                put_l.at[q, ring(row - slot)], got_l.at[q, slot, 0], bl_recv.at[q]
             ).start()
 
     def send_product(q):
         for b in range(near):
             for slot in range(2):
-                src = prod.at[q, slot, :, pl.ds(b * qi, qi), :]
-                dst = back.at[q, channels(row - slot)]
+                src = prod.at[q, slot, b]
+                dst = back.at[q, ring(row - slot)]
                 if b == 0:
                     pltpu.make_async_copy(src, dst, p_recv.at[q]).start()
                 else:
@@ -298,22 +287,36 @@
 
     wait(vall, sem_v.at[3])
     fill_pick(jnp.max(vall[...], axis=0))
-    wait(got_r.at[:, :, pl.ds(0, (nr - near + 1) * ti), :], f_recv)
-
-    def pack(t, carry):
-        p = pl.multiple_of(t * 256, 256)
-        for slot in range(2):
+    wait(got_r.at[:, pl.ds(0, nr - near + 1)], f_recv)
+    loop(0, nq, lambda q: wait(put_r.at[0], b_send.at[0, q]))
+
+    blocks = nq // dc
+    for slot in range(2):
+
+        def split(r):
+            rows = got_r[slot, r].astype(F32).reshape(nq, dc, qi, VALID)
             for n in range(dc):
-                packed_r[slot, n, pl.ds(p, 256), :] = dot(pick[pl.ds(p, 256), :], got_r[slot, n]).astype(BF)
-        return carry
-
-    lax.fori_loop(0, VALID // 256, pack, 0)
+                put_r[n * blocks + r] = rows[:, n].reshape(ti, VALID).astype(BF).reshape(nr, dc * qi, VALID)
+
+        def pack(t):
+            p = pl.multiple_of(t * 256, 256)
+            for n in range(dc):
+                rows = put_r[n * blocks:(n + 1) * blocks].reshape(nr * ti, VALID)
+                packed_r[slot, n, pl.ds(p, 256), :] = dot(pick[pl.ds(p, 256), :], rows).astype(BF)
+
+        loop(0, nr, split)
+        loop(0, VALID // 256, pack)
+
+    which = lax.broadcasted_iota(jnp.int32, (near * dc * qi, VALID), 0) // qi % dc
 
     def product(q):
         wait(got_l.at[q], bl_recv.at[q])
         for slot in range(2):
-            for n in range(dc):
-                prod[q, slot, n] = dot_t(got_l[q, slot, n], packed_r[slot, n]).astype(BF)
+            rows = got_l[q, slot].reshape(near * dc * qi, VALID)
+            out = dot_t(rows, packed_r[slot, 0])
+            for n in range(1, dc):
+                out = jnp.where(which == n, dot_t(rows, packed_r[slot, n]), out)
+            prod[q, slot] = out.astype(BF).reshape(near, dc * qi, VALID)
         send_product(q)
 
     loop(0, nq, product)
@@ -324,15 +327,10 @@
         wait(send_r.at[pl.ds(0, qi * (nc - 1) // nc)], a_send.at[0, q])
         wait(back.at[q], p_recv.at[q])
 
-        def body(t, carry):
-            i = pl.multiple_of(q * qi + t * 16, 16)
-            a = back[q, :, pl.ds(pl.multiple_of(t * 16, 16), 16), :].reshape(16 * cc, VALID)
-            e = dot(dot(perm[...], a).astype(BF), pick[...]).astype(BF)
-            for n in range(nc):
-                send_l[pl.ds(i, 16), n * cc:(n + 1) * cc, :] = e[:, n * tk:(n + 1) * tk].reshape(16, cc, tk)
-            return carry
-
-        lax.fori_loop(0, qi // 16, body, 0)
+        a = back[q].reshape(cc * qi, VALID)
+        e = dot(dot(perm[1], a).astype(BF), pick[...]).astype(BF)
+        for n in range(nc):
+            send_l[part, n * cc:(n + 1) * cc, :] = e[:, n * tk:(n + 1) * tk].reshape(qi, cc, tk)
         dst = field.at[part, pl.ds(pl.multiple_of(col * cc, cc), cc), :]
         for d in range(1, nc):
             to = col_peer(d)
@@ -368,10 +366,9 @@
     wait(vall.at[pl.ds(0, nr - 1)], sem_v.at[2])
 
     def finish(q):
-        wait(put_r.at[pl.ds(0, dc * 2 * near), pl.ds(0, qi), :], b_send.at[0, q])
-        wait(got_r.at[:, :, pl.ds(0, (near - 1) * qi), :], f_send.at[q])
-        wait(put_l.at[pl.ds(0, dc * 2 * (near - 1)), pl.ds(0, qi), :], b_send.at[1, q])
-        wait(prod.at[0, :, :, pl.ds(0, (near - 1) * qi), :], p_send.at[q])
+        wait(put_r.at[0, pl.ds(0, 2 * (near - 1))], f_send.at[q])
+        wait(put_l.at[0, pl.ds(0, 2 * (near - 1))], b_send.at[1, q])
+        wait(prod.at[0, :, pl.ds(0, near - 1)], p_send.at[q])
         wait(send_l.at[pl.ds(0, qi * (nc - 1) // nc)], e_send.at[q])
         out_copy(q).wait()
 
@@ -380,7 +377,7 @@
 
 def solution(mesh):
     nr, nc = mesh.shape["row"], mesh.shape["col"]
-    nq = 8
+    nq = 16
 
     def on_device(pair_rep, pair_mask, w_left_gate, w_left_proj, w_right_gate, w_right_proj, w_gate, w_out):
         ti, tk, cz = pair_rep.shape
@@ -398,16 +395,16 @@
             scratch_shapes=[
                 tile, tile, tile, tile,
                 pltpu.VMEM((ti, cc, nc * tk), BF), pltpu.VMEM((ti, cc, nc * tk), BF),
-                pltpu.VMEM((cc, ti, VALID), BF), pltpu.VMEM((cc, ti, VALID), BF),
-                pltpu.VMEM((2, dc, nr * ti, VALID), BF), pltpu.VMEM((nq, 2, dc, nr // 2 * qi, VALID), BF),
+                pltpu.VMEM((nq, nr, dc * qi, VALID), BF), pltpu.VMEM((nq, nr, dc * qi, VALID), BF),
+                pltpu.VMEM((2, nr, nq, dc * qi, VALID), BF), pltpu.VMEM((nq, 2, nr // 2, dc * qi, VALID), BF),
                 pltpu.VMEM((2, dc, VALID, VALID), BF),
-                pltpu.VMEM((nq, 2, dc, nr // 2 * qi, VALID), BF),
-                pltpu.VMEM((nq, cc, qi, VALID), BF),
+                pltpu.VMEM((nq, 2, nr // 2, dc * qi, VALID), BF),
+                pltpu.VMEM((nq, nr, dc * qi, VALID), BF),
                 pltpu.VMEM((VALID, nc * tk), BF),
                 pltpu.VMEM((6, ch, cz), BF),
                 pltpu.VMEM((ti, tk), F32), pltpu.VMEM((8, tk), F32),
                 pltpu.VMEM((8, nc * tk), F32), pltpu.VMEM((nr, 8, nc * tk), F32),
-                pltpu.VMEM((16 * cc, 16 * cc), BF), pltpu.VMEM((ch, ch), BF),
+                pltpu.VMEM((2, qi * cc, qi * cc), BF), pltpu.VMEM((ch, ch), BF),
                 sem((nq,)), sem((nq,)), sem((4,)), sem((2, nq)), sem((2, nq)), sem((2, nq)),
                 sem((nq,)), sem((nq,)), sem(()), sem((nq,)), sem((nq,)), sem((nq,)), sem((nq,)), sem((nq,)),
             ],

time: 231 us -> 223 us (0.965); the launches traced: 227 us -> 223 us
  Pallas kernels: 222 us -> 218 us
    pallas_call x1, Pallas kernels: 222 us -> 218 us  [on_device(): pl.pallas_call(functools.partial(kernel, nr, nc, nq), out_shape=jax.Shape...]
where the time goes in v4:
time: 223 us
  Pallas kernels  218 us (98%)
  local copies, waits for them, and re-layouts  4.79 us (2%)
    pallas_call x1, Pallas kernels, on_device(): pl.pallas_call(functools.partial(kernel, nr, nc, nq), out_shape=jax.Shape...  218 us
    unnamed x1, local copies, waits for them, and re-layouts  4.79 us

profile of v4, /device:TPU:4, one launch (start us, length us, event | category | flops | bytes accessed | tf_op | source)
XLA Modules:
  0.0 222.8 jit_solution(10840252399727593557)
XLA Ops:
  0.0 218.0 %shard_map.82 = bf16[128,128,128]{2,1,0:T(8,128)(2,1)} custom-call(bf16[128,128,128]{2,1,0:T(8,128)(2,1)} %x_hbm.1, s32[128,128]{1,0:T(8,128)} %mask_ref.1, bf16[128,128]{1,0:T(8,128)(2,1)} %wlg_ref.1, bf16[128,128]{1,0:T(8,128)(2,1)} %wlp_ref.1, bf16[128,128]{1,0:T(8,128)(2,1)} %wrg_ref.1, bf16[128,128]{1,0:T(8,128)(2,1)} %wrp_ref.1, ...), custom_call_target="tpu_custom_call" | custom-call | tf_op jit(solution)/shard_map/pallas_call | solution.py:390
  218.1 4.8 %copy.10 = bf16[128,128,128]{2,1,0:T(8,128)(2,1)} copy(bf16[128,128,128]{2,1,0:T(8,128)(2,1)} %shard_map.82) | data formatting | bytes 8388608

commit v5 on v4

--- a/solution.py
+++ b/solution.py
@@ -38,22 +38,23 @@
 
 def kernel(
     nr, nc, nq,
-    x_hbm, mask_ref, wlg_ref, wlp_ref, wrg_ref, wrp_ref, wg_ref, wo_ref,
+    x_hbm, mask_hbm, wlg_hbm, wlp_hbm, wrg_hbm, wrp_hbm, wg_hbm, wo_hbm,
     out_hbm,
     field, normed, send_r, send_l, recv_r, recv_l, put_r, put_l, got_r, got_l,
-    packed_r, prod, back, pick, w_t, maskf, vmine, vrow, vall, perm, eye,
-    sem_x, sem_out, sem_v, a_send, a_recv, b_send, br_recv, f_send, f_recv, bl_recv, p_send, p_recv, e_send, e_recv,
+    packed_r, prod, back, pick, w_in, w_t, mask_in, maskf, vmine, vrow, vall, perm, eye,
+    sem_in, sem_x, sem_out, sem_v, a_send, a_recv, b_send, br_recv, f_send, f_recv, bl_recv, p_send, p_recv, e_send, e_recv,
 ):
     row = lax.axis_index("row")
     col = lax.axis_index("col")
-    ti, tk = mask_ref.shape
+    ti, tk = mask_in.shape
     ch = w_t.shape[1]
     cc = ch // nc
     dc = cc // nr
     qi = ti // nq
     full = nc * tk
     near = nr // 2
-    ahead = nq // 2
+    ahead = nq // 4
+    behind = nq // 2
     lag = 2
     group = 8
 
@@ -70,9 +71,6 @@
     def out_copy(q):
         part = pl.ds(pl.multiple_of(q * qi, qi), qi)
         return pltpu.make_async_copy(send_r.at[part], out_hbm.at[part], sem_out.at[q])
-
-    for q in range(nq):
-        x_copy(q).start()
 
     barrier = pltpu.get_barrier_semaphore()
     for d in range(1, nc):
@@ -80,16 +78,26 @@
     for d in range(1, nr):
         pl.semaphore_signal(barrier, inc=1, device_id={"row": row_peer(d)}, device_id_type=MESH)
 
+    weights = (wrg_hbm, wrp_hbm, wlg_hbm, wlp_hbm, wg_hbm, wo_hbm)
+    w_copy = [pltpu.make_async_copy(ref, w_in.at[n], sem_in.at[n]) for n, ref in enumerate(weights)]
+    mask_copy = pltpu.make_async_copy(mask_hbm, mask_in, sem_in.at[len(weights)])
+    x_copy(0).start()
+    for copy in w_copy[:2] + [mask_copy] + w_copy[2:]:
+        copy.start()
+    for q in range(1, nq):
+        x_copy(q).start()
+
+    def turn(n):
+        w_copy[n].wait()
+        w_t[n] = dot_t(eye[...], w_in[n]).astype(BF)
+
     eye[...] = (
         lax.broadcasted_iota(jnp.int32, (ch, ch), 0) == lax.broadcasted_iota(jnp.int32, (ch, ch), 1)
     ).astype(F32).astype(BF)
-    at = lax.broadcasted_iota(jnp.int32, (cc * qi, cc * qi), 0)
-    of = lax.broadcasted_iota(jnp.int32, (cc * qi, cc * qi), 1)
-    perm[0] = (of == (at % qi) * cc + at // qi).astype(F32).astype(BF)
-    perm[1] = (at == (of % qi) * cc + of // qi).astype(F32).astype(BF)
-    for n, ref in enumerate((wrg_ref, wrp_ref, wlg_ref, wlp_ref, wg_ref, wo_ref)):
-        w_t[n] = dot_t(eye[...], ref[...]).astype(BF)
-    maskf[...] = mask_ref[...].astype(F32)
+    turn(0)
+    turn(1)
+    mask_copy.wait()
+    maskf[...] = mask_in[...].astype(F32)
     vmine[...] = jnp.broadcast_to(jnp.max(maskf[...], axis=0, keepdims=True), vmine.shape)
 
     mine = pl.ds(pl.multiple_of(col * tk, tk), tk)
@@ -244,6 +252,13 @@
         ).start()
     pltpu.make_async_copy(vmine, vrow.at[:, mine], sem_v.at[1]).start()
 
+    for n in range(2, len(weights)):
+        turn(n)
+    at = lax.broadcasted_iota(jnp.int32, (cc * qi, cc * qi), 0)
+    of = lax.broadcasted_iota(jnp.int32, (cc * qi, cc * qi), 1)
+    perm[0] = (of == (at % qi) * cc + at // qi).astype(F32).astype(BF)
+    perm[1] = (at == (of % qi) * cc + of // qi).astype(F32).astype(BF)
+
     def next_r(q):
         x_copy(q).wait()
         compute_r(q)
@@ -280,10 +295,13 @@
         compact(1, q, recv_l, put_l)
         send_left(q)
 
-    loop(0, nq - ahead, across_r, lambda q: next_r(q + ahead))
-    loop(nq - ahead, nq, across_r, lambda q: next_l(q - ahead), lambda q: forward_right(q - ahead))
-    loop(0, nq - ahead, across_l, lambda q: next_l(q + ahead), lambda q: forward_right(q + ahead))
-    loop(nq - ahead, nq, across_l)
+    edge = nq - ahead
+    loop(0, behind, across_r, lambda q: next_r(q + ahead))
+    loop(behind, edge, across_r, lambda q: next_r(q + ahead), lambda q: forward_right(q - behind))
+    loop(edge, nq, across_r, lambda q: next_l(q - edge), lambda q: forward_right(q - behind))
+    loop(0, nq - behind, across_l, lambda q: next_l(q + ahead), lambda q: forward_right(q + behind))
+    loop(nq - behind, edge, across_l, lambda q: next_l(q + ahead))
+    loop(edge, nq, across_l)
 
     wait(vall, sem_v.at[3])
     fill_pick(jnp.max(vall[...], axis=0))
@@ -386,11 +404,10 @@
         qi = ti // nq
         tile = pltpu.VMEM((ti, ch, tk), BF)
         sem = pltpu.SemaphoreType.DMA
-        vmem = pl.BlockSpec(memory_space=pltpu.VMEM)
         return pl.pallas_call(
             functools.partial(kernel, nr, nc, nq),
             out_shape=jax.ShapeDtypeStruct(pair_rep.shape, pair_rep.dtype),
-            in_specs=[pl.BlockSpec(memory_space=pl.ANY)] + [vmem] * 7,
+            in_specs=[pl.BlockSpec(memory_space=pl.ANY)] * 8,
             out_specs=pl.BlockSpec(memory_space=pl.ANY),
             scratch_shapes=[
                 tile, tile, tile, tile,
@@ -401,11 +418,11 @@
                 pltpu.VMEM((nq, 2, nr // 2, dc * qi, VALID), BF),
                 pltpu.VMEM((nq, nr, dc * qi, VALID), BF),
                 pltpu.VMEM((VALID, nc * tk), BF),
-                pltpu.VMEM((6, ch, cz), BF),
-                pltpu.VMEM((ti, tk), F32), pltpu.VMEM((8, tk), F32),
+                pltpu.VMEM((6, ch, cz), BF), pltpu.VMEM((6, ch, cz), BF),
+                pltpu.VMEM((ti, tk), jnp.int32), pltpu.VMEM((ti, tk), F32), pltpu.VMEM((8, tk), F32),
                 pltpu.VMEM((8, nc * tk), F32), pltpu.VMEM((nr, 8, nc * tk), F32),
                 pltpu.VMEM((2, qi * cc, qi * cc), BF), pltpu.VMEM((ch, ch), BF),
-                sem((nq,)), sem((nq,)), sem((4,)), sem((2, nq)), sem((2, nq)), sem((2, nq)),
+                sem((7,)), sem((nq,)), sem((nq,)), sem((4,)), sem((2, nq)), sem((2, nq)), sem((2, nq)),
                 sem((nq,)), sem((nq,)), sem(()), sem((nq,)), sem((nq,)), sem((nq,)), sem((nq,)), sem((nq,)),
             ],
             compiler_params=pltpu.CompilerParams(

time: 223 us -> 222 us (level)
  no operation moved by 1% of the time
where the time goes in v5:
time: 222 us
  Pallas kernels  217 us (98%)
  local copies, waits for them, and re-layouts  4.79 us (2%)
    pallas_call x1, Pallas kernels, on_device(): pl.pallas_call(functools.partial(kernel, nr, nc, nq), out_shape=jax.Shape...  217 us
    unnamed x1, local copies, waits for them, and re-layouts  4.79 us

profile of v5, /device:TPU:4, one launch (start us, length us, event | category | flops | bytes accessed | tf_op | source)
XLA Modules:
  0.0 222.1 jit_solution(5298172594475410821)
XLA Ops:
  0.0 217.3 %shard_map.82 = bf16[128,128,128]{2,1,0:T(8,128)(2,1)} custom-call(bf16[128,128,128]{2,1,0:T(8,128)(2,1)} %x_hbm.1, s32[128,128]{1,0:T(8,128)} %mask_hbm.1, bf16[128,128]{1,0:T(8,128)(2,1)} %wlg_hbm.1, bf16[128,128]{1,0:T(8,128)(2,1)} %wlp_hbm.1, bf16[128,128]{1,0:T(8,128)(2,1)} %wrg_hbm.1, bf16[128,128]{1,0:T(8,128)(2,1)} %wrp_hbm.1, ...), custom_call_target="tpu_custom_call" | custom-call | tf_op jit(solution)/shard_map/pallas_call | solution.py:407
  217.3 4.8 %copy.10 = bf16[128,128,128]{2,1,0:T(8,128)(2,1)} copy(bf16[128,128,128]{2,1,0:T(8,128)(2,1)} %shard_map.82) | data formatting | bytes 8388608

commit v6 on v5

--- a/solution.py
+++ b/solution.py
@@ -243,14 +243,14 @@
     x_copy(0).wait()
     compute_r(0)
     pl.semaphore_wait(barrier, nc - 1 + nr - 1)
-    start_a(0, 0, send_r, recv_r)
-
     for d in range(1, nc):
         pltpu.make_async_remote_copy(
             vmine, vrow.at[:, mine], sem_v.at[0], sem_v.at[1],
             device_id={"col": col_peer(d)}, device_id_type=MESH,
         ).start()
     pltpu.make_async_copy(vmine, vrow.at[:, mine], sem_v.at[1]).start()
+
+    start_a(0, 0, send_r, recv_r)
 
     for n in range(2, len(weights)):
         turn(n)
@@ -393,6 +393,21 @@
     loop(0, nq, finish)
 
 
+def hand_over(src, dst, held, sem_in, sem_out):
+    parts = sem_in.shape[0]
+    size = src.shape[0] // parts
+    pieces = [pl.ds(n * size, size) for n in range(parts)]
+    reads = [pltpu.make_async_copy(src.at[p], held.at[p], sem_in.at[n]) for n, p in enumerate(pieces)]
+    writes = [pltpu.make_async_copy(held.at[p], dst.at[p], sem_out.at[n]) for n, p in enumerate(pieces)]
+    for read in reads:
+        read.start()
+    for read, write in zip(reads, writes):
+        read.wait()
+        write.start()
+    for write in writes:
+        write.wait()
+
+
 def solution(mesh):
     nr, nc = mesh.shape["row"], mesh.shape["col"]
     nq = 16
@@ -404,7 +419,7 @@
         qi = ti // nq
         tile = pltpu.VMEM((ti, ch, tk), BF)
         sem = pltpu.SemaphoreType.DMA
-        return pl.pallas_call(
+        update = pl.pallas_call(
             functools.partial(kernel, nr, nc, nq),
             out_shape=jax.ShapeDtypeStruct(pair_rep.shape, pair_rep.dtype),
             in_specs=[pl.BlockSpec(memory_space=pl.ANY)] * 8,
@@ -429,6 +444,14 @@
                 collective_id=0, has_side_effects=True, vmem_limit_bytes=58 << 20
             ),
         )(pair_rep, pair_mask, w_left_gate, w_left_proj, w_right_gate, w_right_proj, w_gate, w_out)
+        return pl.pallas_call(
+            hand_over,
+            out_shape=jax.ShapeDtypeStruct(pair_rep.shape, pair_rep.dtype),
+            in_specs=[pl.BlockSpec(memory_space=pl.ANY)],
+            out_specs=pl.BlockSpec(memory_space=pl.ANY),
+            scratch_shapes=[pltpu.VMEM(pair_rep.shape, pair_rep.dtype), sem((8,)), sem((8,))],
+            compiler_params=pltpu.CompilerParams(vmem_limit_bytes=56 << 20),
+        )(update)
 
     in_specs = (P(("dp", "row"), "col", None), P(("dp", "row"), "col")) + (P(),) * 6
     return jax.shard_map(

time: 222 us -> 219 us (0.986)
  local copies, waits for them, and re-layouts: 4.79 us -> 0 us
    unnamed x1 -> x0, local copies, waits for them, and re-layouts: 4.79 us -> none
    pallas_call x0 -> x1, Pallas kernels: none -> 3.58 us  [on_device(): pl.pallas_call(hand_over, out_shape=jax.ShapeDtypeStruct(pair_rep.shape,...]
where the time goes in v6:
time: 219 us
  Pallas kernels  219 us (100%)
    pallas_call x1, Pallas kernels, on_device(): pl.pallas_call(functools.partial(kernel, nr, nc, nq), out_shape=jax.Shape...  215 us

profile of v6, /device:TPU:4, one launch (start us, length us, event | category | flops | bytes accessed | tf_op | source)
XLA Modules:
  0.0 218.7 jit_solution(9306912819558819963)
XLA Ops:
  0.0 215.1 %shard_map.82.src = bf16[128,128,128]{2,1,0:T(8,128)(2,1)} custom-call(bf16[128,128,128]{2,1,0:T(8,128)(2,1)} %x_hbm.1, s32[128,128]{1,0:T(8,128)} %mask_hbm.1, bf16[128,128]{1,0:T(8,128)(2,1)} %wlg_hbm.1, bf16[128,128]{1,0:T(8,128)(2,1)} %wlp_hbm.1, bf16[128,128]{1,0:T(8,128)(2,1)} %wrg_hbm.1, bf16[128,128]{1,0:T(8,128)(2,1)} %wrp_hbm.1, ...), custom_call_target="tpu_custom_call" | custom-call | tf_op jit(solution)/shard_map/pallas_call | solution.py:422
  215.1 3.6 %shard_map.83 = bf16[128,128,128]{2,1,0:T(8,128)(2,1)} custom-call(bf16[128,128,128]{2,1,0:T(8,128)(2,1)} %shard_map.82.src), custom_call_target="tpu_custom_call" | custom-call | tf_op jit(solution)/shard_map/pallas_call | solution.py:447

commit v7 on v6

--- a/solution.py
+++ b/solution.py
@@ -41,7 +41,7 @@
     x_hbm, mask_hbm, wlg_hbm, wlp_hbm, wrg_hbm, wrp_hbm, wg_hbm, wo_hbm,
     out_hbm,
     field, normed, send_r, send_l, recv_r, recv_l, put_r, put_l, got_r, got_l,
-    packed_r, prod, back, pick, w_in, w_t, mask_in, maskf, vmine, vrow, vall, perm, eye,
+    packed_r, prod, back, pick, w_in, w_t, mask_in, maskf, vmine, vrow, vpack, vall, perm, eye,
     sem_in, sem_x, sem_out, sem_v, a_send, a_recv, b_send, br_recv, f_send, f_recv, bl_recv, p_send, p_recv, e_send, e_recv,
 ):
     row = lax.axis_index("row")
@@ -279,13 +279,15 @@
     loop(1, ahead, next_r)
 
     wait(vrow, sem_v.at[1])
-    fill_pick(vrow[...])
+    for n in range(nc):
+        vpack[n:n + 1, :] = vrow[0:1, n * tk:(n + 1) * tk]
     for d in range(1, nr):
         pltpu.make_async_remote_copy(
-            vrow, vall.at[row], sem_v.at[2], sem_v.at[3],
+            vpack, vall.at[row], sem_v.at[2], sem_v.at[3],
             device_id={"row": row_peer(d)}, device_id_type=MESH,
         ).start()
-    pltpu.make_async_copy(vrow, vall.at[row], sem_v.at[3]).start()
+    pltpu.make_async_copy(vpack, vall.at[row], sem_v.at[3]).start()
+    fill_pick(vrow[...])
 
     def across_r(q):
         compact(0, q, recv_r, put_r)
@@ -304,7 +306,8 @@
     loop(edge, nq, across_l)
 
     wait(vall, sem_v.at[3])
-    fill_pick(jnp.max(vall[...], axis=0))
+    valid = jnp.max(vall[...], axis=0)
+    fill_pick(jnp.concatenate([jnp.broadcast_to(valid[n:n + 1, :], vmine.shape) for n in range(nc)], axis=1))
     wait(got_r.at[:, pl.ds(0, nr - near + 1)], f_recv)
     loop(0, nq, lambda q: wait(put_r.at[0], b_send.at[0, q]))
 
@@ -435,7 +438,7 @@
                 pltpu.VMEM((VALID, nc * tk), BF),
                 pltpu.VMEM((6, ch, cz), BF), pltpu.VMEM((6, ch, cz), BF),
                 pltpu.VMEM((ti, tk), jnp.int32), pltpu.VMEM((ti, tk), F32), pltpu.VMEM((8, tk), F32),
-                pltpu.VMEM((8, nc * tk), F32), pltpu.VMEM((nr, 8, nc * tk), F32),
+                pltpu.VMEM((8, nc * tk), F32), pltpu.VMEM((nc, tk), F32), pltpu.VMEM((nr, nc, tk), F32),
                 pltpu.VMEM((2, qi * cc, qi * cc), BF), pltpu.VMEM((ch, ch), BF),
                 sem((7,)), sem((nq,)), sem((nq,)), sem((4,)), sem((2, nq)), sem((2, nq)), sem((2, nq)),
                 sem((nq,)), sem((nq,)), sem(()), sem((nq,)), sem((nq,)), sem((nq,)), sem((nq,)), sem((nq,)),

time: 219 us -> 216 us (0.986)
  Pallas kernels: 219 us -> 216 us
    pallas_call x1, Pallas kernels: 215 us -> 213 us  [on_device(): pl.pallas_call(functools.partial(kernel, nr, nc, nq), out_shape=jax.Shape...]
where the time goes in v7:
time: 216 us
  Pallas kernels  216 us (100%)
    pallas_call x1, Pallas kernels, on_device(): pl.pallas_call(functools.partial(kernel, nr, nc, nq), out_shape=jax.Shape...  213 us

profile of v7, /device:TPU:4, one launch (start us, length us, event | category | flops | bytes accessed | tf_op | source)
XLA Modules:
  0.0 216.2 jit_solution(13901993625573595349)
XLA Ops:
  0.0 212.6 %shard_map.82.src = bf16[128,128,128]{2,1,0:T(8,128)(2,1)} custom-call(bf16[128,128,128]{2,1,0:T(8,128)(2,1)} %x_hbm.1, s32[128,128]{1,0:T(8,128)} %mask_hbm.1, bf16[128,128]{1,0:T(8,128)(2,1)} %wlg_hbm.1, bf16[128,128]{1,0:T(8,128)(2,1)} %wlp_hbm.1, bf16[128,128]{1,0:T(8,128)(2,1)} %wrg_hbm.1, bf16[128,128]{1,0:T(8,128)(2,1)} %wrp_hbm.1, ...), custom_call_target="tpu_custom_call" | custom-call | tf_op jit(solution)/shard_map/pallas_call | solution.py:425
  212.6 3.6 %shard_map.83 = bf16[128,128,128]{2,1,0:T(8,128)(2,1)} custom-call(bf16[128,128,128]{2,1,0:T(8,128)(2,1)} %shard_map.82.src), custom_call_target="tpu_custom_call" | custom-call | tf_op jit(solution)/shard_map/pallas_call | solution.py:450

commit v8 on v7

--- a/solution.py
+++ b/solution.py
@@ -53,6 +53,7 @@
     qi = ti // nq
     full = nc * tk
     near = nr // 2
+    far_first = sorted(range(1, nc), key=lambda d: -min(d % (nc // 2), -d % (nc // 2)))
     ahead = nq // 4
     behind = nq // 2
     lag = 2
@@ -135,7 +136,7 @@
 
     def start_a(n, q, src, dst):
         part = pl.ds(pl.multiple_of(q * qi, qi), qi)
-        for d in range(1, nc):
+        for d in far_first:
             to = col_peer(d)
             pltpu.make_async_remote_copy(
                 src.at[part, pl.ds(pl.multiple_of(to * cc, cc), cc), :], dst.at[part, :, mine],
@@ -156,7 +157,7 @@
         dst[q] = b.reshape(nr, dc * qi, VALID)
 
     def start_near(piece, send, recv):
-        for b in range(1, near):
+        for b in range(near - 1, 0, -1):
             for slot_at, d in ((0, b), (1, -b)):
                 src, dst = piece(slot_at, b)
                 pltpu.make_async_remote_copy(
@@ -202,7 +203,7 @@
             ).start()
 
     def send_product(q):
-        for b in range(near):
+        for b in range(near - 1, -1, -1):
             for slot in range(2):
                 src = prod.at[q, slot, b]
                 dst = back.at[q, ring(row - slot)]
@@ -353,7 +354,7 @@
         for n in range(nc):
             send_l[part, n * cc:(n + 1) * cc, :] = e[:, n * tk:(n + 1) * tk].reshape(qi, cc, tk)
         dst = field.at[part, pl.ds(pl.multiple_of(col * cc, cc), cc), :]
-        for d in range(1, nc):
+        for d in far_first:
             to = col_peer(d)
             pltpu.make_async_remote_copy(
                 send_l.at[part, pl.ds(pl.multiple_of(to * cc, cc), cc), :], dst,

time: 216 us -> 216 us (level)
  no operation moved by 1% of the time
where the time goes in v8:
time: 216 us
  Pallas kernels  216 us (100%)
    pallas_call x1, Pallas kernels, on_device(): pl.pallas_call(functools.partial(kernel, nr, nc, nq), out_shape=jax.Shape...  212 us

profile of v8, /device:TPU:4, one launch (start us, length us, event | category | flops | bytes accessed | tf_op | source)
XLA Modules:
  0.0 215.6 jit_solution(6229091859288967186)
XLA Ops:
  0.0 212.1 %shard_map.82.src = bf16[128,128,128]{2,1,0:T(8,128)(2,1)} custom-call(bf16[128,128,128]{2,1,0:T(8,128)(2,1)} %x_hbm.1, s32[128,128]{1,0:T(8,128)} %mask_hbm.1, bf16[128,128]{1,0:T(8,128)(2,1)} %wlg_hbm.1, bf16[128,128]{1,0:T(8,128)(2,1)} %wlp_hbm.1, bf16[128,128]{1,0:T(8,128)(2,1)} %wrg_hbm.1, bf16[128,128]{1,0:T(8,128)(2,1)} %wrp_hbm.1, ...), custom_call_target="tpu_custom_call" | custom-call | tf_op jit(solution)/shard_map/pallas_call | solution.py:426
  212.1 3.6 %shard_map.83 = bf16[128,128,128]{2,1,0:T(8,128)(2,1)} custom-call(bf16[128,128,128]{2,1,0:T(8,128)(2,1)} %shard_map.82.src), custom_call_target="tpu_custom_call" | custom-call | tf_op jit(solution)/shard_map/pallas_call | solution.py:451

commit v9 on v7

--- a/solution.py
+++ b/solution.py
@@ -452,7 +452,7 @@
             out_shape=jax.ShapeDtypeStruct(pair_rep.shape, pair_rep.dtype),
             in_specs=[pl.BlockSpec(memory_space=pl.ANY)],
             out_specs=pl.BlockSpec(memory_space=pl.ANY),
-            scratch_shapes=[pltpu.VMEM(pair_rep.shape, pair_rep.dtype), sem((8,)), sem((8,))],
+            scratch_shapes=[pltpu.VMEM(pair_rep.shape, pair_rep.dtype), sem((16,)), sem((16,))],
             compiler_params=pltpu.CompilerParams(vmem_limit_bytes=56 << 20),
         )(update)
 

time: 216 us -> 217 us (level)
  no operation moved by 1% of the time
where the time goes in v9:
time: 217 us; the launch traced here: 216 us
  Pallas kernels  216 us (100%)
    pallas_call x1, Pallas kernels, on_device(): pl.pallas_call(functools.partial(kernel, nr, nc, nq), out_shape=jax.Shape...  213 us

profile of v9, /device:TPU:4, one launch (start us, length us, event | category | flops | bytes accessed | tf_op | source)
XLA Modules:
  0.0 216.4 jit_solution(15457710258483701480)
XLA Ops:
  0.0 212.6 %shard_map.82.src = bf16[128,128,128]{2,1,0:T(8,128)(2,1)} custom-call(bf16[128,128,128]{2,1,0:T(8,128)(2,1)} %x_hbm.1, s32[128,128]{1,0:T(8,128)} %mask_hbm.1, bf16[128,128]{1,0:T(8,128)(2,1)} %wlg_hbm.1, bf16[128,128]{1,0:T(8,128)(2,1)} %wlp_hbm.1, bf16[128,128]{1,0:T(8,128)(2,1)} %wrg_hbm.1, bf16[128,128]{1,0:T(8,128)(2,1)} %wrp_hbm.1, ...), custom_call_target="tpu_custom_call" | custom-call | tf_op jit(solution)/shard_map/pallas_call | solution.py:425
  212.6 3.9 %shard_map.83 = bf16[128,128,128]{2,1,0:T(8,128)(2,1)} custom-call(bf16[128,128,128]{2,1,0:T(8,128)(2,1)} %shard_map.82.src), custom_call_target="tpu_custom_call" | custom-call | tf_op jit(solution)/shard_map/pallas_call | solution.py:450
